TPU v7x, 512 devices: a whole 4x4x16 slice. The times are simulated.
512 devices in a mesh: dp: 4 (over x_lo, core), neg: 128 (over x_hi, y, z).
Axes of the slice: x: 4 (x_hi: 2, x_lo: 2; x = x_hi * 2 + x_lo), y: 4, z: 16, core: 2. Of those that a mesh axis runs over, the one named last changes fastest.
Arguments:
- queries: bfloat16 [262144, 1024], P(('dp', 'neg')), parts along dimension 0, may hold values from -48 to 48
- passages: bfloat16 [262144, 1024], P(('dp', 'neg')), parts along dimension 0, may hold values from -8 to 8
- partners: int32 [2, 128], replicated, may hold values from 0 to 127, as said below
- positives: int32 [262144], P(('dp', 'neg')), parts along dimension 0, may hold values from 0 to 511
Outputs:
- row_loss: float32 [262144], P(('dp', 'neg')), parts along dimension 0
- grad_queries: bfloat16 [262144, 1024], P(('dp', 'neg')), parts along dimension 0
- grad_passages: bfloat16 [262144, 1024], P(('dp', 'neg')), parts along dimension 0
There are 4 independent parts, one for each index of `dp`. A program takes and returns all parts, laid end to end along the dimension named above; an argument that names none is the same for every part. Nothing has to cross between parts.
Inputs may be any that keep to these rules, and one draw needn't show every extreme that they name: `partners`: in each round r the table maps block b to b XOR 2**k_r, with a different k_r in each round, so each round pairs the blocks; one of the rounds pairs b with b XOR 128/2.
All inputs are finite; a program needn't handle non-finite values.
Results may differ from a plain program's by a relative error of at most 0.0034.
Values may be sent and summed in bfloat16 or wider, within the bound.
A program may use at most 64 MiB of HBM per device.

v0:
```python
from functools import partial

import jax
import jax.numpy as jnp
from jax import lax
from jax.sharding import PartitionSpec as P


def as_sent(array):
    return jax.tree.map(lambda a: a.astype(jnp.bfloat16) if a.dtype == jnp.float32 else a, array)


def swapped(value, axis, stride):
    mask = 2**stride
    pairs = [(source, source ^ mask) for source in range(lax.axis_size(axis))]
    return lax.ppermute(value, axis, pairs)


def tile_scores(left, right, scale):
    return (
        lax.dot_general(left, right, (((1,), (1,)), ((), ())), preferred_element_type=jnp.float32)
        * scale
    )


def tile_back(weights, rows):
    return lax.dot_general(
        weights, rows, (((0,), (0,)), ((), ())), preferred_element_type=jnp.float32
    )


def which_bit(value, levels):
    places = jnp.arange(levels, dtype=jnp.int32)
    return jnp.sum(jnp.where(jnp.right_shift(value, places) % 2 == 1, places, 0))


def send_blocks(value, bit):
    return jax.tree.map(
        lambda part, own: part.astype(own.dtype), swapped(as_sent(value), "neg", bit), value
    )


def send_back(value, bit):
    return jax.tree.map(
        lambda part, own: part.astype(own.dtype), swapped(as_sent(value), "neg", bit), value
    )


def by_bit(mover, value, index, levels):
    branches = [partial(mover, bit=level) for level in range(levels)]
    return lax.switch(index, branches, value)


def per_device(queries, passages, partners, positives):
    rows, width = queries.shape
    scale = width ** (-0.5)
    levels = lax.axis_size("neg").bit_length() - 1
    rounds = partners.shape[0]
    bits = [which_bit(partners[r, 0], levels) for r in range(rounds)]
    columns = jnp.arange(rows, dtype=jnp.int32)
    hit = positives[:, None] == columns[None, :]
    blocks = [passages] + [by_bit(send_blocks, passages, bits[r], levels) for r in range(rounds)]
    scores = [tile_scores(queries, block, scale) for block in blocks]
    top = scores[0].max(axis=1)
    for tile in scores[1:]:
        top = jnp.maximum(top, tile.max(axis=1))
    total = jnp.zeros_like(top)
    for tile in scores:
        total = total + jnp.sum(jnp.exp(tile - top[:, None]), axis=1)
    lse = top + jnp.log(total)
    row_loss = lse - jnp.sum(jnp.where(hit, scores[0], 0.0), axis=1)
    weights = []
    for k, tile in enumerate(scores):
        prob = jnp.exp(tile - lse[:, None])
        if k == 0:
            prob = prob - hit.astype(jnp.float32)
        weights.append(prob.astype(jnp.bfloat16))
    grad_query = jnp.zeros((rows, width), jnp.float32)
    for wtile, block in zip(weights, blocks):
        grad_query = grad_query + jnp.dot(wtile, block, preferred_element_type=jnp.float32)
    summed = tile_back(weights[0], queries)
    for r in range(rounds):
        mine = tile_back(weights[r + 1], queries).astype(jnp.bfloat16)
        piece = by_bit(send_back, mine, bits[r], levels)
        summed = summed + piece.astype(jnp.float32)
    return (row_loss, grad_query.astype(jnp.bfloat16), summed.astype(jnp.bfloat16))


def solution(mesh):
    placed = (P(("dp", "neg"), None), P(("dp", "neg"), None), P(), P(("dp", "neg")))
    return jax.shard_map(
        per_device,
        mesh=mesh,
        in_specs=placed,
        out_specs=(P(("dp", "neg")), P(("dp", "neg"), None), P(("dp", "neg"), None)),
        check_vma=False,
    )
```

profile of v0, /device:TPU:24, one launch (start us, length us, event | category | flops | bytes accessed | tf_op | source)
XLA Modules:
  0.0 130.5 jit_solution(11869152519746126880)
XLA Ops:
  0.6 0.0 copy-start
  0.6 1.3 fusion.7
  1.9 1.3 fusion.3
  3.9 1.3 fusion.4
  5.8 27.1 %conditional.10 = (bf16[512,1024]{1,0:T(8,128)(2,1)}) conditional(s32[]{:T(128)} %clamp.8, bf16[512,1024]{1,0:T(8,128)(2,1)} %param.33, bf16[512,1024]{1,0:T(8,128)(2,1)} %param.33, bf16[512,1024]{1,0:T(8,128)(2,1)} %param.33, bf16[512,1024]{1,0:T(8,128)(2,1)} %param.33, bf16[512,1024]{1,0:T(8,128)(2,1)} %param.33, ...), branch_computations={%region_2.3_spmd, %region_3.4_spmd, %region_4.5_spmd, %region_5.6_... | conditional | bytes 4194352 | solution.py:51
  5.8 2.7 %collective-permute-start.4 = (bf16[512,1024]{1,0:T(8,128)(2,1)}, bf16[512,1024]{1,0:T(8,128)(2,1)}, u32[]{:S(2)}, u32[]{:S(2)}) collective-permute-start(bf16[512,1024]{1,0:T(8,128)(2,1)} %param.4), channel_id=1, source_target_pairs={{0,16},{1,17},{2,18},{3,19},{4,20},{5,21},{6,22},{7,23},{8,24},{9,... | collective-permute-start | bytes 3145736 | tf_op jit(solution)/shard_map/cond/branch_4_fun/ppermute | solution.py:16
  8.5 24.4 %collective-permute-done.4 = bf16[512,1024]{1,0:T(8,128)(2,1)} collective-permute-done((bf16[512,1024]{1,0:T(8,128)(2,1)}, bf16[512,1024]{1,0:T(8,128)(2,1)}, u32[]{:S(2)}, u32[]{:S(2)}) %collective-permute-start.4) | collective-permute-done | bytes 1048608 | tf_op jit(solution)/shard_map/cond/branch_4_fun/ppermute | solution.py:16
  33.0 27.7 %conditional.11 = (bf16[512,1024]{1,0:T(8,128)(2,1)}) conditional(s32[]{:T(128)} %clamp.9, bf16[512,1024]{1,0:T(8,128)(2,1)} %param.33, bf16[512,1024]{1,0:T(8,128)(2,1)} %param.33, bf16[512,1024]{1,0:T(8,128)(2,1)} %param.33, bf16[512,1024]{1,0:T(8,128)(2,1)} %param.33, bf16[512,1024]{1,0:T(8,128)(2,1)} %param.33, ...), branch_computations={%region_11.12_spmd, %region_12.13_spmd, %region_13.14_spmd, %regio... | conditional | bytes 4194352 | solution.py:51
  33.0 4.9 %collective-permute-start.13 = (bf16[512,1024]{1,0:T(8,128)(2,1)}, bf16[512,1024]{1,0:T(8,128)(2,1)}, u32[]{:S(2)}, u32[]{:S(2)}) collective-permute-start(bf16[512,1024]{1,0:T(8,128)(2,1)} %param.13), channel_id=1, source_target_pairs={{0,64},{1,65},{2,66},{3,67},{4,68},{5,69},{6,70},{7,71},{8,72},{9,... | collective-permute-start | bytes 3145736 | tf_op jit(solution)/shard_map/cond/branch_6_fun/ppermute | solution.py:16
  37.9 22.8 %collective-permute-done.13 = bf16[512,1024]{1,0:T(8,128)(2,1)} collective-permute-done((bf16[512,1024]{1,0:T(8,128)(2,1)}, bf16[512,1024]{1,0:T(8,128)(2,1)}, u32[]{:S(2)}, u32[]{:S(2)}) %collective-permute-start.13) | collective-permute-done | bytes 1048608 | tf_op jit(solution)/shard_map/cond/branch_6_fun/ppermute | solution.py:16
  60.7 0.0 copy-done
  60.7 2.0 %fusion.8 = (f32[512]{0:T(512)S(1)}, f32[512,512]{0,1:T(8,128)S(1)}) fusion(bf16[512,1024]{1,0:T(8,128)(2,1)} %get-tuple-element.90, bf16[512,1024]{1,0:T(8,128)(2,1)S(1)} %copy-done), kind=kOutput, calls=%fused_computation.33 | convolution fusion | flops 537394688 | bytes 3147776 | tf_op jit(solution)/shard_map/dot_general | solution.py:21
  62.7 0.0 copy-start.3
  62.8 0.0 copy-start.7
  62.8 2.5 %fusion.10 = (f32[512]{0:T(512)S(1)}, f32[512,512]{0,1:T(8,128)S(1)}) fusion(bf16[512,1024]{1,0:T(8,128)(2,1)} %get-tuple-element.89, bf16[512,1024]{1,0:T(8,128)(2,1)S(1)} %copy-done), kind=kOutput, calls=%fused_computation.35 | convolution fusion | flops 537394688 | bytes 3147776 | tf_op jit(solution)/shard_map/dot_general | solution.py:21
  65.2 0.0 copy-start.6
  65.2 0.0 copy-start.9
  65.2 0.0 copy-done.7
  65.2 0.8 fusion.9
  66.0 0.0 copy-start.1
  66.0 0.0 copy-done.3
  66.0 0.0 copy-done.9
  66.1 0.8 select_reduce_fusion
  66.8 0.6 fusion.6
  67.4 0.0 copy-done.6
  67.4 0.9 convolution_convert_fusion.1
  68.3 0.0 copy-done.1
  68.3 25.1 %conditional.12 = (bf16[512,1024]{1,0:T(8,128)(2,1)}) conditional(s32[]{:T(128)} %clamp.8, bf16[512,1024]{1,0:T(8,128)(2,1)S(1)} %convolution_convert_fusion.1, bf16[512,1024]{1,0:T(8,128)(2,1)S(1)} %convolution_convert_fusion.1, bf16[512,1024]{1,0:T(8,128)(2,1)S(1)} %convolution_convert_fusion.1, ...), branch_computations={%region_23.24_spmd, %region_24.25_spmd, %region_25.26_spmd, %regio... | conditional | bytes 4194352
  68.3 2.7 %collective-permute-start.18 = (bf16[512,1024]{1,0:T(8,128)(2,1)S(1)}, bf16[512,1024]{1,0:T(8,128)(2,1)}, u32[]{:S(2)}, u32[]{:S(2)}) collective-permute-start(bf16[512,1024]{1,0:T(8,128)(2,1)S(1)} %param.18), channel_id=1, source_target_pairs={{0,16},{1,17},{2,18},{3,19},{4,20},{5,21},{6,22},{7,23},{8,24},{9,... | collective-permute-start | bytes 3145736 | tf_op jit(solution)/shard_map/cond/branch_4_fun/ppermute | solution.py:16
  71.0 22.5 %collective-permute-done.18 = bf16[512,1024]{1,0:T(8,128)(2,1)} collective-permute-done((bf16[512,1024]{1,0:T(8,128)(2,1)S(1)}, bf16[512,1024]{1,0:T(8,128)(2,1)}, u32[]{:S(2)}, u32[]{:S(2)}) %collective-permute-start.18) | collective-permute-done | bytes 1048608 | tf_op jit(solution)/shard_map/cond/branch_4_fun/ppermute | solution.py:16
  93.4 0.0 copy-start.4
  93.4 2.4 %fusion.5 = f32[512,1024]{1,0:T(8,128)S(1)} fusion(bf16[512,1024]{1,0:T(8,128)(2,1)} %get-tuple-element.89, f32[512,512]{0,1:T(8,128)} %copy-done.6, f32[512]{0:T(512)S(1)} %get-tuple-element.80), kind=kOutput, calls=%fused_computation.30 | convolution fusion | flops 537395200 | bytes 4196352 | tf_op jit(solution)/shard_map/dot_general | solution.py:80
  95.8 0.0 copy-done.4
  95.9 0.8 convolution_convert_fusion
  96.7 25.7 %conditional.13 = (bf16[512,1024]{1,0:T(8,128)(2,1)}) conditional(s32[]{:T(128)} %clamp.9, bf16[512,1024]{1,0:T(8,128)(2,1)S(1)} %convolution_convert_fusion, bf16[512,1024]{1,0:T(8,128)(2,1)S(1)} %convolution_convert_fusion, bf16[512,1024]{1,0:T(8,128)(2,1)S(1)} %convolution_convert_fusion, ...), branch_computations={%region_30.31_spmd, %region_31.32_spmd, %region_32.33_spmd, %regio... | conditional | bytes 4194352
  96.7 4.9 %collective-permute-start.27 = (bf16[512,1024]{1,0:T(8,128)(2,1)S(1)}, bf16[512,1024]{1,0:T(8,128)(2,1)}, u32[]{:S(2)}, u32[]{:S(2)}) collective-permute-start(bf16[512,1024]{1,0:T(8,128)(2,1)S(1)} %param.27), channel_id=1, source_target_pairs={{0,64},{1,65},{2,66},{3,67},{4,68},{5,69},{6,70},{7,71},{8,72},{9,... | collective-permute-start | bytes 3145736 | tf_op jit(solution)/shard_map/cond/branch_6_fun/ppermute | solution.py:16
  101.7 20.8 %collective-permute-done.27 = bf16[512,1024]{1,0:T(8,128)(2,1)} collective-permute-done((bf16[512,1024]{1,0:T(8,128)(2,1)S(1)}, bf16[512,1024]{1,0:T(8,128)(2,1)}, u32[]{:S(2)}, u32[]{:S(2)}) %collective-permute-start.27) | collective-permute-done | bytes 1048608 | tf_op jit(solution)/shard_map/cond/branch_6_fun/ppermute | solution.py:16
  122.4 0.0 copy-start.2
  122.4 0.0 copy-start.8
  122.4 3.8 %add_convert_fusion = bf16[512,1024]{1,0:T(8,128)(2,1)} fusion(bf16[512,1024]{1,0:T(8,128)(2,1)} %get-tuple-element.92, bf16[512,1024]{1,0:T(8,128)(2,1)} %get-tuple-element.91, bf16[512,1024]{1,0:T(8,128)(2,1)S(1)} %copy-done, f32[512,512]{0,1:T(8,128)} %copy-done.1, f32[512]{0:T(512)S(1)} %get-tuple-element.80, s32[512]{0:T(512)S(1)} %copy-done.9), kind=kOutput, calls=%fused_computation | convolution fusion | flops 540803072 | bytes 5246976 | tf_op jit(solution)/shard_map/dot_general | solution.py:27
  126.2 0.0 copy-done.2
  126.2 0.0 copy-done.8
  126.2 0.0 copy-start.5
  126.2 0.8 fusion
  127.0 0.4 copy-done.5
  127.5 3.0 %add_convert_fusion.1 = bf16[512,1024]{1,0:T(8,128)(2,1)} fusion(f32[512,1024]{1,0:T(8,128)S(1)} %fusion, f32[512,1024]{1,0:T(8,128)S(1)} %fusion.5, bf16[512,1024]{1,0:T(8,128)(2,1)} %get-tuple-element.90, f32[512,512]{0,1:T(8,128)S(1)} %copy-done.5, f32[512]{0:T(512)S(1)} %get-tuple-element.80), kind=kOutput, calls=%fused_computation.1 | convolution fusion | flops 538968064 | bytes 7342080 | tf_op jit(solution)/shard_map/dot_general | solution.py:80
  (1 shorter events, 0.0 us)
Async XLA Ops:
  0.6 60.1 %copy-start = (bf16[512,1024]{1,0:T(8,128)(2,1)S(1)}, bf16[512,1024]{1,0:T(8,128)(2,1)}, u32[]{:S(2)}) copy-start(bf16[512,1024]{1,0:T(8,128)(2,1)} %param.32) | copy-start | bytes 3145732
  5.8 27.1 %collective-permute-start.4 = (bf16[512,1024]{1,0:T(8,128)(2,1)}, bf16[512,1024]{1,0:T(8,128)(2,1)}, u32[]{:S(2)}, u32[]{:S(2)}) collective-permute-start(bf16[512,1024]{1,0:T(8,128)(2,1)} %param.4), channel_id=1, source_target_pairs={{0,16},{1,17},{2,18},{3,19},{4,20},{5,21},{6,22},{7,23},{8,24},{9,... | collective-permute-start | bytes 3145736 | tf_op jit(solution)/shard_map/cond/branch_4_fun/ppermute | solution.py:16
  33.0 27.7 %collective-permute-start.13 = (bf16[512,1024]{1,0:T(8,128)(2,1)}, bf16[512,1024]{1,0:T(8,128)(2,1)}, u32[]{:S(2)}, u32[]{:S(2)}) collective-permute-start(bf16[512,1024]{1,0:T(8,128)(2,1)} %param.13), channel_id=1, source_target_pairs={{0,64},{1,65},{2,66},{3,67},{4,68},{5,69},{6,70},{7,71},{8,72},{9,... | collective-permute-start | bytes 3145736 | tf_op jit(solution)/shard_map/cond/branch_6_fun/ppermute | solution.py:16
  62.7 3.3 %copy-start.3 = (f32[512,512]{0,1:T(8,128)}, f32[512,512]{0,1:T(8,128)S(1)}, u32[]{:S(2)}) copy-start(f32[512,512]{0,1:T(8,128)S(1)} %get-tuple-element.84) | copy-start | bytes 3145732
  62.8 2.5 %copy-start.7 = (bf16[512,1024]{1,0:T(8,128)(2,1)S(1)}, bf16[512,1024]{1,0:T(8,128)(2,1)}, u32[]{:S(2)}) copy-start(bf16[512,1024]{1,0:T(8,128)(2,1)} %param.33) | copy-start | bytes 3145732
  65.2 2.2 %copy-start.6 = (f32[512,512]{0,1:T(8,128)}, f32[512,512]{0,1:T(8,128)S(1)}, u32[]{:S(2)}) copy-start(f32[512,512]{0,1:T(8,128)S(1)} %get-tuple-element.88) | copy-start | bytes 3145732
  65.2 0.8 copy-start.9
  66.0 2.3 %copy-start.1 = (f32[512,512]{0,1:T(8,128)}, f32[512,512]{0,1:T(8,128)S(1)}, u32[]{:S(2)}) copy-start(f32[512,512]{0,1:T(8,128)S(1)} %get-tuple-element.86) | copy-start | bytes 3145732
  68.3 25.1 %collective-permute-start.18 = (bf16[512,1024]{1,0:T(8,128)(2,1)S(1)}, bf16[512,1024]{1,0:T(8,128)(2,1)}, u32[]{:S(2)}, u32[]{:S(2)}) collective-permute-start(bf16[512,1024]{1,0:T(8,128)(2,1)S(1)} %param.18), channel_id=1, source_target_pairs={{0,16},{1,17},{2,18},{3,19},{4,20},{5,21},{6,22},{7,23},{8,24},{9,... | collective-permute-start | bytes 3145736 | tf_op jit(solution)/shard_map/cond/branch_4_fun/ppermute | solution.py:16
  93.4 2.4 %copy-start.4 = (f32[512,512]{0,1:T(8,128)S(1)}, f32[512,512]{0,1:T(8,128)}, u32[]{:S(2)}) copy-start(f32[512,512]{0,1:T(8,128)} %copy-done.3) | copy-start | bytes 3145732
  96.7 25.7 %collective-permute-start.27 = (bf16[512,1024]{1,0:T(8,128)(2,1)S(1)}, bf16[512,1024]{1,0:T(8,128)(2,1)}, u32[]{:S(2)}, u32[]{:S(2)}) collective-permute-start(bf16[512,1024]{1,0:T(8,128)(2,1)S(1)} %param.27), channel_id=1, source_target_pairs={{0,64},{1,65},{2,66},{3,67},{4,68},{5,69},{6,70},{7,71},{8,72},{9,... | collective-permute-start | bytes 3145736 | tf_op jit(solution)/shard_map/cond/branch_6_fun/ppermute | solution.py:16
  122.4 3.8 %copy-start.2 = (f32[512,512]{0,1:T(8,128)S(1)}, f32[512,512]{0,1:T(8,128)}, u32[]{:S(2)}) copy-start(f32[512,512]{0,1:T(8,128)} %copy-done.1) | copy-start | bytes 3145732
  122.4 3.8 %copy-start.8 = (bf16[512,1024]{1,0:T(8,128)(2,1)S(1)}, bf16[512,1024]{1,0:T(8,128)(2,1)}, u32[]{:S(2)}) copy-start(bf16[512,1024]{1,0:T(8,128)(2,1)} %param.33) | copy-start | bytes 3145732
  126.2 1.2 copy-start.5
where the time goes:
time: 131 us; the launch traced here: 130 us
  waiting for transfers between devices  90.5 us (69%)
  matrix products  16.9 us (13%)
  starting transfers between devices  15.2 us (12%)
  other arithmetic  3.93 us (3%)
  between operations  2.07 us (2%)
  local copies, waits for them, and re-layouts  1.78 us (1%)
    ppermute x4, waiting for transfers between devices, swapped(): return lax.ppermute(value, axis, pairs)  90.5 us
    ppermute x4, starting transfers between devices, swapped(): return lax.ppermute(value, axis, pairs)  15.2 us
    dot_general x3, matrix products, per_device(): jnp.dot(wtile, block, preferred_element_type=jnp.float32)  6.2 us
    dot_general x3, matrix products, tile_back(): lax.dot_general(weights, rows, (((0,), (0,)), ((), ())), preferred_elemen...  5.48 us
    dot_general x3, matrix products, tile_scores(): lax.dot_general(left, right, (((1,), (1,)), ((), ())), preferred_element_...  5.26 us
  transfers between devices with their start and end apart: 4, of which 4 were waited for; matrix products, arithmetic and copies ran while one was open for 0% of the time, Pallas kernels for 0%

commit v1 on v0

v1 whole, which is shorter than its diff:
```python
import functools

import jax
import jax.numpy as jnp
from jax import lax
from jax.experimental import pallas as pl
from jax.experimental.pallas import tpu as pltpu
from jax.sharding import PartitionSpec as P

MESH = pl.DeviceIdType.MESH
CHUNK = 128
EARLY = 2


def nt(left, right):
    return lax.dot_general(left, right, (((1,), (1,)), ((), ())), preferred_element_type=jnp.float32)


def tn(left, right):
    return lax.dot_general(left, right, (((0,), (0,)), ((), ())), preferred_element_type=jnp.float32)


def nn(left, right):
    return jnp.dot(left, right, preferred_element_type=jnp.float32)


def kernel(strides, scale, q_hbm, p_hbm, pos_ref, loss_ref, dq_hbm, dp_hbm,
           q, p, pin, qin, s, w, own, part, outq, outp, lse_own, lse_in,
           load_sem, store_sem, p_send, p_recv, q_send, q_recv, l_send, l_recv):
    rows, width = q.shape
    n = rows // CHUNK
    dp, me = lax.axis_index("dp"), lax.axis_index("neg")
    peers = [(dp, jnp.bitwise_xor(me, stride)) for stride in strides]

    loads = [pltpu.make_async_copy(p_hbm, p, load_sem.at[0]), pltpu.make_async_copy(q_hbm, q, load_sem.at[1])]
    for load in loads:
        load.start()
    barrier = pltpu.get_barrier_semaphore()
    for peer in peers:
        pl.semaphore_signal(barrier, inc=1, device_id=peer, device_id_type=MESH)
    pl.semaphore_wait(barrier, len(peers))

    def part_of(c):
        return pl.ds(pl.multiple_of(c * CHUNK, CHUNK), CHUNK)

    def send(src, dst, send_sem, recv_sem, i, c):
        return pltpu.make_async_remote_copy(
            src_ref=src.at[part_of(c)], dst_ref=dst.at[i, part_of(c)],
            send_sem=send_sem.at[i, c], recv_sem=recv_sem.at[i, c],
            device_id=peers[i], device_id_type=MESH)

    def send_p(i, c):
        return send(p_hbm, pin, p_send, p_recv, i, c)

    def send_q(i, c):
        return send(q_hbm, qin, q_send, q_recv, i, c)

    def send_lse(i):
        return pltpu.make_async_remote_copy(
            src_ref=lse_own, dst_ref=lse_in.at[i], send_sem=l_send.at[i], recv_sem=l_recv.at[i],
            device_id=peers[i], device_id_type=MESH)

    for c in range(n):
        for i in (0, 1):
            send_p(i, c).start()
    for c in range(EARLY):
        for i in (0, 1):
            send_q(i, c).start()

    for load in loads:
        load.wait()

    def scores(k, block, c, top):
        tile = nt(block, q[...]) * scale
        s[k, part_of(c)] = tile
        return jnp.maximum(top, jnp.max(tile.reshape(CHUNK // 8, 8, rows), axis=0))

    def own_scores(c, top):
        return scores(0, p[part_of(c)], c, top)

    top = lax.fori_loop(0, n, own_scores, jnp.full((8, rows), -jnp.inf, jnp.float32))

    def partner_scores(c, top):
        for i in (0, 1):
            send_p(i, c).wait_recv()
            top = scores(i + 1, pin[i, part_of(c)], c, top)
        return top

    top = lax.fori_loop(0, n, partner_scores, top)
    top = jnp.max(top, axis=0, keepdims=True)

    def add_up(c, total):
        for k in range(3):
            tile = jnp.exp(s[k, part_of(c)] - top)
            total = total + jnp.sum(tile.reshape(CHUNK // 8, 8, rows), axis=0)
        return total

    total = lax.fori_loop(0, n, add_up, jnp.zeros((8, rows), jnp.float32))
    lse = top + jnp.log(jnp.sum(total, axis=0, keepdims=True))
    lse_own[...] = jnp.broadcast_to(lse, lse_own.shape)
    for i in (0, 1):
        send_lse(i).start()
    for c in range(EARLY, n):
        for i in (0, 1):
            send_q(i, c).start()

    positive = pos_ref[...]

    def weigh(c, picked):
        tile = s[0, part_of(c)]
        hit = lax.broadcasted_iota(jnp.int32, tile.shape, 0) + c * CHUNK == positive
        picked = picked + jnp.sum(jnp.where(hit, tile, 0.0).reshape(CHUNK // 8, 8, rows), axis=0)
        w[0, part_of(c)] = (jnp.exp(tile - lse) - hit.astype(jnp.float32)).astype(jnp.bfloat16)
        for k in (1, 2):
            w[k, part_of(c)] = jnp.exp(s[k, part_of(c)] - lse).astype(jnp.bfloat16)
        return picked

    picked = lax.fori_loop(0, n, weigh, jnp.zeros((8, rows), jnp.float32))
    loss_ref[...] = lse - jnp.sum(picked, axis=0, keepdims=True)

    def store(src, dst, sem, c):
        return pltpu.make_async_copy(src.at[part_of(c)], dst.at[part_of(c)], sem.at[c])

    def grad_q(c, _):
        grad = tn(w[0, :, part_of(c)], p[...])
        for i in (0, 1):
            grad = grad + tn(w[i + 1, :, part_of(c)], pin[i])
        outq[part_of(c)] = grad.astype(jnp.bfloat16)
        store(outq, dq_hbm, store_sem.at[0], c).start()
        own[part_of(c)] = nn(w[0, part_of(c)], q[...])
        return 0

    lax.fori_loop(0, n, grad_q, 0)
    for i in (0, 1):
        send_lse(i).wait_recv()

    def partner_weights(i, c):
        send_q(i, c).wait_recv()
        tile = nt(p[...], qin[i, part_of(c)]) * scale
        return jnp.exp(tile - lse_in[i, 0:1, part_of(c)]).astype(jnp.bfloat16)

    def partner_back(c, _):
        for i in (0, 1):
            term = nn(partner_weights(i, c), qin[i, part_of(c)])

            @pl.when(c == 0)
            def _():
                part[i] = term

            @pl.when(c > 0)
            def _():
                part[i] += term
        return 0

    lax.fori_loop(0, n - 1, partner_back, 0)
    last = n - 1
    part[0] += nn(partner_weights(0, last), qin[0, part_of(last)])
    own[...] += part[0].astype(jnp.bfloat16).astype(jnp.float32)
    w[0, :, 0:CHUNK] = partner_weights(1, last)

    def finish(c, _):
        mine = part[1, part_of(c)] + nn(w[0, part_of(c), 0:CHUNK], qin[1, part_of(last)])
        outp[part_of(c)] = (own[part_of(c)] + mine.astype(jnp.bfloat16).astype(jnp.float32)).astype(jnp.bfloat16)
        store(outp, dp_hbm, store_sem.at[1], c).start()
        return 0

    lax.fori_loop(0, n, finish, 0)
    for c in range(n):
        for i in (0, 1):
            send_p(i, c).wait_send()
            send_q(i, c).wait_send()
    for i in (0, 1):
        send_lse(i).wait_send()
    for c in range(n):
        store(outq, dq_hbm, store_sem.at[0], c).wait()
        store(outp, dp_hbm, store_sem.at[1], c).wait()


def call(level, half, scale, queries, passages, positives):
    rows, width = queries.shape
    n = rows // CHUNK
    flops = 11 * 2 * rows * rows * width
    vmem, dma = pltpu.VMEM, pltpu.SemaphoreType.DMA
    anywhere = pl.BlockSpec(memory_space=pl.ANY)
    inside = pl.BlockSpec(memory_space=pltpu.VMEM)
    return pl.pallas_call(
        functools.partial(kernel, (half, 2**level), scale),
        out_shape=(
            jax.ShapeDtypeStruct((1, rows), jnp.float32),
            jax.ShapeDtypeStruct((rows, width), jnp.bfloat16),
            jax.ShapeDtypeStruct((rows, width), jnp.bfloat16),
        ),
        in_specs=[anywhere, anywhere, inside],
        out_specs=(inside, anywhere, anywhere),
        scratch_shapes=[
            vmem((rows, width), jnp.bfloat16),
            vmem((rows, width), jnp.bfloat16),
            vmem((2, rows, width), jnp.bfloat16),
            vmem((2, rows, width), jnp.bfloat16),
            vmem((3, rows, rows), jnp.float32),
            vmem((3, rows, rows), jnp.bfloat16),
            vmem((rows, width), jnp.float32),
            vmem((2, rows, width), jnp.float32),
            vmem((rows, width), jnp.bfloat16),
            vmem((rows, width), jnp.bfloat16),
            vmem((8, rows), jnp.float32),
            vmem((2, 8, rows), jnp.float32),
            dma((2,)),
            dma((2, n)),
            dma((2, n)),
            dma((2, n)),
            dma((2, n)),
            dma((2, n)),
            dma((2,)),
            dma((2,)),
        ],
        name=f"exchange_{level}",
        cost_estimate=pl.CostEstimate(flops=flops, bytes_accessed=8 * rows * width, transcendentals=8 * rows * rows),
        compiler_params=pltpu.CompilerParams(
            collective_id=level, has_side_effects=True, vmem_limit_bytes=48 * 2**20),
    )(queries, passages, positives)


def per_device(queries, passages, partners, positives):
    rows, width = queries.shape
    size = lax.axis_size("neg")
    half = size // 2
    other = partners[0, 0] ^ partners[1, 0] ^ half
    levels = half.bit_length() - 1
    index = sum((other >= 2**j).astype(jnp.int32) for j in range(1, levels))
    branches = [functools.partial(call, level, half, width ** (-0.5)) for level in range(levels)]
    loss, grad_queries, grad_passages = lax.switch(index, branches, queries, passages, positives.reshape(1, rows))
    return loss.reshape(rows), grad_queries, grad_passages


def solution(mesh):
    placed = (P(("dp", "neg"), None), P(("dp", "neg"), None), P(), P(("dp", "neg")))
    return jax.shard_map(
        per_device,
        mesh=mesh,
        in_specs=placed,
        out_specs=(P(("dp", "neg")), P(("dp", "neg"), None), P(("dp", "neg"), None)),
        check_vma=False,
    )
```

time: 131 us -> 207 us (1.58)
  the two profiles are of different devices: /device:TPU:24 before, /device:TPU:120 now
where the time goes in v1:
time: 207 us
  Pallas kernels  201 us (97%)
  local copies, waits for them, and re-layouts  4.38 us (2%)
    pallas_call x1, Pallas kernels, call(): pl.pallas_call(functools.partial(kernel, (half, 2 ** level), scale), out_...  201 us

profile of v1, /device:TPU:120, one launch (start us, length us, event | category | flops | bytes accessed | tf_op | source)
XLA Modules:
  0.0 207.2 jit_solution(11501173909333723497)
XLA Ops:
  0.6 0.0 copy-start
  0.6 0.7 copy-done
  1.3 0.5 fusion
  3.1 0.0 copy-start.1
  3.2 0.7 copy-done.1
  3.8 200.9 %conditional.1 = (bf16[512,1024]{1,0:T(8,128)(2,1)S(1)}, bf16[512,1024]{1,0:T(8,128)(2,1)S(1)}, f32[512]{0:T(512)S(1)}) conditional(s32[]{:T(128)} %bitcast.6, (bf16[512,1024]{1,0:T(8,128)(2,1)}, bf16[512,1024]{1,0:T(8,128)(2,1)}, s32[1,512]{1,0:T(1,128)S(1)}) %tuple.49, (bf16[512,1024]{1,0:T(8,128)(2,1)}, ...), branch_computations={%region_0.0_spmd, %region_1.0_spmd, %region_2.0_spmd, %region_3.0_... | conditional | flops 5905580032 | bytes 4194328 | solution.py:232
  3.8 200.6 %exchange_3.1 = (f32[1,512]{1,0:T(1,128)S(1)}, bf16[512,1024]{1,0:T(8,128)(2,1)S(1)}, bf16[512,1024]{1,0:T(8,128)(2,1)S(1)}) custom-call(bf16[512,1024]{1,0:T(8,128)(2,1)} %get-tuple-element.73.q_hbm, bf16[512,1024]{1,0:T(8,128)(2,1)} %get-tuple-element.74.p_hbm, s32[1,512]{1,0:T(1,128)S(1)} %get-tuple-element.75.pos_ref), custom_call_target="tpu_custom_call" | custom-call | flops 5905580032 | bytes 4194304 | tf_op jit(solution)/shard_map/cond/branch_3_fun/exchange_3/pallas_call | solution.py:186
  204.7 0.6 copy.28
  205.3 1.0 copy.29
  206.3 1.0 copy.30
Async XLA Ops:
  0.6 0.7 copy-start
  3.1 0.7 copy-start.1

commit v2 on v1

v2 whole, which is shorter than its diff:
```python
import functools

import jax
import jax.numpy as jnp
from jax import lax
from jax.experimental import pallas as pl
from jax.experimental.pallas import tpu as pltpu
from jax.sharding import PartitionSpec as P

MESH = pl.DeviceIdType.MESH
CHUNK = 128
EARLY = 2


def nt(left, right):
    return lax.dot_general(left, right, (((1,), (1,)), ((), ())), preferred_element_type=jnp.float32)


def tn(left, right):
    return lax.dot_general(left, right, (((0,), (0,)), ((), ())), preferred_element_type=jnp.float32)


def nn(left, right):
    return jnp.dot(left, right, preferred_element_type=jnp.float32)


def exchange(strides, scale, q_hbm, p_hbm, pos_hbm, loss_ref, dq_ref, dp_ref,
             q, pos, allp, qin, s0, sp, w0, wp, own, part, w, lse_own, lse_in,
             load_sem, p_send, p_recv, q_send, q_recv, l_send, l_recv):
    rows, width = q.shape
    n = rows // CHUNK
    pair = 2 * CHUNK
    dp, me = lax.axis_index("dp"), lax.axis_index("neg")
    peers = [(dp, jnp.bitwise_xor(me, stride)) for stride in strides]

    loads = [
        pltpu.make_async_copy(p_hbm, allp.at[pl.ds(0, rows)], load_sem.at[0]),
        pltpu.make_async_copy(q_hbm, q, load_sem.at[1]),
        pltpu.make_async_copy(pos_hbm, pos, load_sem.at[2]),
    ]
    for load in loads:
        load.start()
    barrier = pltpu.get_barrier_semaphore()
    for peer in peers:
        pl.semaphore_signal(barrier, inc=1, device_id=peer, device_id_type=MESH)
    pl.semaphore_wait(barrier, len(peers))

    def chunk(c):
        return pl.ds(pl.multiple_of(c * CHUNK, CHUNK), CHUNK)

    def send_p(i, c):
        at = pl.multiple_of(rows + c * pair + i * CHUNK, CHUNK)
        return pltpu.make_async_remote_copy(
            src_ref=p_hbm.at[chunk(c)], dst_ref=allp.at[pl.ds(at, CHUNK)],
            send_sem=p_send.at[i, c], recv_sem=p_recv.at[i, c], device_id=peers[i], device_id_type=MESH)

    def send_q(i, c):
        return pltpu.make_async_remote_copy(
            src_ref=q_hbm.at[chunk(c)], dst_ref=qin.at[c, pl.ds(i * CHUNK, CHUNK)],
            send_sem=q_send.at[i, c], recv_sem=q_recv.at[i, c], device_id=peers[i], device_id_type=MESH)

    def send_lse(i):
        return pltpu.make_async_remote_copy(
            src_ref=lse_own, dst_ref=lse_in.at[i], send_sem=l_send.at[i], recv_sem=l_recv.at[i],
            device_id=peers[i], device_id_type=MESH)

    for c in range(n):
        for i in (0, 1):
            send_p(i, c).start()
    for c in range(EARLY):
        for i in (0, 1):
            send_q(i, c).start()
    for load in loads:
        load.wait()

    def fold(tile, combine):
        return combine(tile.reshape(tile.shape[0] // 8, 8, rows), axis=0)

    def own_scores(c, top):
        tile = nt(allp[chunk(c)], q[...]) * scale
        s0[chunk(c)] = tile
        return jnp.maximum(top, fold(tile, jnp.max))

    top = lax.fori_loop(0, n, own_scores, jnp.full((8, rows), -jnp.inf, jnp.float32))

    def partner_scores(c, top):
        for i in (0, 1):
            send_p(i, c).wait_recv()
        tile = nt(allp[pl.ds(pl.multiple_of(rows + c * pair, pair), pair)], q[...]) * scale
        sp[c] = tile
        return jnp.maximum(top, fold(tile, jnp.max))

    top = lax.fori_loop(0, n, partner_scores, top)
    top = jnp.max(top, axis=0, keepdims=True)

    def add_up(c, total):
        return total + fold(jnp.exp(s0[chunk(c)] - top), jnp.sum) + fold(jnp.exp(sp[c] - top), jnp.sum)

    total = lax.fori_loop(0, n, add_up, jnp.zeros((8, rows), jnp.float32))
    lse = top + jnp.log(jnp.sum(total, axis=0, keepdims=True))
    lse_own[...] = jnp.broadcast_to(lse, lse_own.shape)
    for i in (0, 1):
        send_lse(i).start()
    for c in range(EARLY, n):
        for i in (0, 1):
            send_q(i, c).start()

    positive = pos[...]

    def weigh(c, picked):
        tile = s0[chunk(c)]
        hit = lax.broadcasted_iota(jnp.int32, tile.shape, 0) + c * CHUNK == positive
        picked = picked + fold(jnp.where(hit, tile, 0.0), jnp.sum)
        w0[chunk(c)] = (jnp.exp(tile - lse) - hit.astype(jnp.float32)).astype(jnp.bfloat16)
        wp[pl.ds(pl.multiple_of(c * pair, pair), pair)] = jnp.exp(sp[c] - lse).astype(jnp.bfloat16)
        return picked

    picked = lax.fori_loop(0, n, weigh, jnp.zeros((8, rows), jnp.float32))
    loss_ref[...] = lse - jnp.sum(picked, axis=0, keepdims=True)

    def local_grads(c, _):
        grad = tn(w0[:, chunk(c)], allp[pl.ds(0, rows)]) + tn(wp[:, chunk(c)], allp[pl.ds(rows, 2 * rows)])
        dq_ref[chunk(c)] = grad.astype(jnp.bfloat16)
        own[chunk(c)] = nn(w0[chunk(c)], q[...])
        return 0

    lax.fori_loop(0, n, local_grads, 0)
    for i in (0, 1):
        send_lse(i).wait_recv()

    def partner_weights(c):
        for i in (0, 1):
            send_q(i, c).wait_recv()
        tile = nt(allp[pl.ds(0, rows)], qin[c]) * scale
        lses = jnp.concatenate([lse_in[i, 0:1, chunk(c)] for i in (0, 1)], axis=1)
        w[...] = jnp.exp(tile - lses).astype(jnp.bfloat16)

    halves = [pl.ds(i * CHUNK, CHUNK) for i in (0, 1)]

    def partner_back(c, first):
        partner_weights(c)

        def columns(j, _):
            span = pl.ds(pl.multiple_of(j * 256, 256), 256)
            for i in (0, 1):
                term = nn(w[:, halves[i]], qin[c, halves[i], span])
                part[i, :, span] = term if first else part[i, :, span] + term
            return 0

        lax.fori_loop(0, width // 256, columns, 0)

    partner_back(0, True)

    def more(c, _):
        partner_back(c, False)
        return 0

    lax.fori_loop(1, n - 1, more, 0)
    partner_weights(n - 1)

    def finish(c, _):
        big = pl.ds(pl.multiple_of(c * 256, 256), 256)
        total = own[big]
        for i in (0, 1):
            mine = part[i, big] + nn(w[big, halves[i]], qin[n - 1, halves[i]])
            total = total + mine.astype(jnp.bfloat16).astype(jnp.float32)
        dp_ref[big] = total.astype(jnp.bfloat16)
        return 0

    lax.fori_loop(0, 2, finish, 0)
    for c in range(n):
        for i in (0, 1):
            send_p(i, c).wait_send()
            send_q(i, c).wait_send()
    for i in (0, 1):
        send_lse(i).wait_send()


def call_exchange(level, half, scale, queries, passages, positives):
    rows, width = queries.shape
    n = rows // CHUNK
    vmem, dma = pltpu.VMEM, pltpu.SemaphoreType.DMA
    f32, bf16 = jnp.float32, jnp.bfloat16
    outside = pl.BlockSpec(memory_space=pltpu.HBM)
    inside = pl.BlockSpec(memory_space=pltpu.VMEM)
    return pl.pallas_call(
        functools.partial(exchange, (half, 2**level), scale),
        out_shape=(vmem((1, rows), f32), vmem((rows, width), bf16), vmem((rows, width), bf16)),
        in_specs=[outside] * 3,
        out_specs=(inside,) * 3,
        scratch_shapes=[
            vmem((rows, width), bf16),
            vmem((1, rows), jnp.int32),
            vmem((3 * rows, width), bf16),
            vmem((n, 2 * CHUNK, width), bf16),
            vmem((rows, rows), f32),
            vmem((n, 2 * CHUNK, rows), f32),
            vmem((rows, rows), bf16),
            vmem((2 * rows, rows), bf16),
            vmem((rows, width), f32),
            vmem((2, rows, width), f32),
            vmem((rows, 2 * CHUNK), bf16),
            vmem((8, rows), f32),
            vmem((2, 8, rows), f32),
            dma((3,)),
            dma((2, n)),
            dma((2, n)),
            dma((2, n)),
            dma((2, n)),
            dma((2,)),
            dma((2,)),
        ],
        name=f"exchange_{level}",
        cost_estimate=pl.CostEstimate(
            flops=22 * rows * rows * width, bytes_accessed=8 * rows * width, transcendentals=8 * rows * rows),
        compiler_params=pltpu.CompilerParams(
            collective_id=level, has_side_effects=True, vmem_limit_bytes=32 * 2**20),
    )(queries, passages, positives)


def write_out(loss, dq, dp, loss_hbm, dq_hbm, dp_hbm, sem):
    n = dq.shape[0] // CHUNK
    copies = [pltpu.make_async_copy(loss, loss_hbm, sem.at[2 * n])]
    for c in range(n):
        block = pl.ds(c * CHUNK, CHUNK)
        copies.append(pltpu.make_async_copy(dq.at[block], dq_hbm.at[block], sem.at[c]))
        copies.append(pltpu.make_async_copy(dp.at[block], dp_hbm.at[block], sem.at[n + c]))
    for copy in copies:
        copy.start()
    for copy in copies:
        copy.wait()


def call_write_out(*parts):
    outside = pl.BlockSpec(memory_space=pltpu.HBM)
    inside = pl.BlockSpec(memory_space=pltpu.VMEM)
    return pl.pallas_call(
        write_out,
        out_shape=tuple(jax.ShapeDtypeStruct(part.shape, part.dtype) for part in parts),
        in_specs=[inside] * 3,
        out_specs=(outside,) * 3,
        scratch_shapes=[pltpu.SemaphoreType.DMA((2 * (parts[1].shape[0] // CHUNK) + 1,))],
        name="write_out",
        compiler_params=pltpu.CompilerParams(vmem_limit_bytes=8 * 2**20),
    )(*parts)


def choose(half, levels, partners, index):
    other = partners[0, 0] ^ partners[1, 0] ^ half
    place = jnp.int32(0)
    for j in range(1, levels):
        place = place + (other >= 2**j).astype(jnp.int32)
    index[0] = place


def call_choose(half, levels, partners):
    return pl.pallas_call(
        functools.partial(choose, half, levels),
        out_shape=pltpu.SMEM((1,), jnp.int32),
        in_specs=[pl.BlockSpec(memory_space=pltpu.SMEM)],
        out_specs=pl.BlockSpec(memory_space=pltpu.SMEM),
        name="choose",
    )(partners)


def per_device(queries, passages, partners, positives):
    rows, width = queries.shape
    half = lax.axis_size("neg") // 2
    levels = half.bit_length() - 1
    index = call_choose(half, levels, partners)[0]
    branches = [functools.partial(call_exchange, level, half, width ** (-0.5)) for level in range(levels)]
    parts = lax.switch(index, branches, queries, passages, positives.reshape(1, rows))
    loss, grad_queries, grad_passages = call_write_out(*parts)
    return loss.reshape(rows), grad_queries, grad_passages


def solution(mesh):
    placed = (P(("dp", "neg"), None), P(("dp", "neg"), None), P(), P(("dp", "neg")))
    return jax.shard_map(
        per_device,
        mesh=mesh,
        in_specs=placed,
        out_specs=(P(("dp", "neg")), P(("dp", "neg"), None), P(("dp", "neg"), None)),
        check_vma=False,
    )
```

time: 207 us -> 198 us (0.957)
  the two profiles are of different devices: /device:TPU:120 before, /device:TPU:24 now
where the time goes in v2:
time: 198 us
  Pallas kernels  197 us (99%)
    pallas_call x1, Pallas kernels, call_exchange(): pl.pallas_call(functools.partial(exchange, (half, 2 ** level), scale), ou...  194 us

profile of v2, /device:TPU:24, one launch (start us, length us, event | category | flops | bytes accessed | tf_op | source)
XLA Modules:
  0.0 198.3 jit_solution(7375754862949141777)
XLA Ops:
  0.6 0.7 choose.1
  1.3 0.0 copy-start
  1.4 0.7 copy-done
  2.0 194.7 %conditional.1 = ((f32[1,512]{1,0:T(1,128)S(1)}, bf16[512,1024]{1,0:T(8,128)(2,1)S(1)}, bf16[512,1024]{1,0:T(8,128)(2,1)S(1)})) conditional(s32[]{:T(128)} %bitcast, (bf16[512,1024]{1,0:T(8,128)(2,1)}, bf16[512,1024]{1,0:T(8,128)(2,1)}, s32[1,512]{1,0:T(1,128)S(1)}) %tuple.40, (bf16[512,1024]{1,0:T(8,128)(2,1)}, ...), branch_computations={%region_0.0_spmd, %region_1.0_spmd, %region_2.0_spmd, %region_3.0_... | conditional | flops 5905580032 | bytes 4194312 | solution.py:272
  2.0 194.5 %exchange_2.1 = (f32[1,512]{1,0:T(1,128)S(1)}, bf16[512,1024]{1,0:T(8,128)(2,1)S(1)}, bf16[512,1024]{1,0:T(8,128)(2,1)S(1)}) custom-call(bf16[512,1024]{1,0:T(8,128)(2,1)} %get-tuple-element.42.q_hbm, bf16[512,1024]{1,0:T(8,128)(2,1)} %get-tuple-element.43.p_hbm, s32[1,512]{1,0:T(1,128)S(1)} %get-tuple-element.44.pos_hbm), custom_call_target="tpu_custom_call" | custom-call | flops 5905580032 | bytes 4194304 | tf_op jit(solution)/shard_map/cond/branch_2_fun/exchange_2/pallas_call | solution.py:186
  196.7 1.4 write_out.1
Async XLA Ops:
  1.3 0.7 copy-start

commit v3 on v2

v3 whole, which is shorter than its diff:
```python
import functools

import jax
import jax.numpy as jnp
from jax import lax
from jax.experimental import pallas as pl
from jax.experimental.pallas import tpu as pltpu
from jax.sharding import PartitionSpec as P

MESH = pl.DeviceIdType.MESH
TILE = 128
EARLY = 2
FIN = 256


def nt(left, right):
    return lax.dot_general(left, right, (((1,), (1,)), ((), ())), preferred_element_type=jnp.float32)


def tn(left, right):
    return lax.dot_general(left, right, (((0,), (0,)), ((), ())), preferred_element_type=jnp.float32)


def nn(left, right):
    return jnp.dot(left, right, preferred_element_type=jnp.float32)


def exchange(strides, scale, q_hbm, p_hbm, pos_hbm, loss_ref, dq_ref, dp_ref,
             q, pos, allp, qin, s, w, w_in, own, lse_own, lse_in,
             load_sem, p_send, p_recv, q_send, q_recv, l_send, l_recv):
    rows, width = q.shape
    n = rows // TILE
    dp, me = lax.axis_index("dp"), lax.axis_index("neg")
    peers = [(dp, jnp.bitwise_xor(me, stride)) for stride in strides]

    loads = [
        pltpu.make_async_copy(p_hbm, allp.at[pl.ds(0, rows)], load_sem.at[0]),
        pltpu.make_async_copy(q_hbm, q, load_sem.at[1]),
        pltpu.make_async_copy(pos_hbm, pos, load_sem.at[2]),
    ]
    for load in loads:
        load.start()
    barrier = pltpu.get_barrier_semaphore()
    for peer in peers:
        pl.semaphore_signal(barrier, inc=1, device_id=peer, device_id_type=MESH)
    pl.semaphore_wait(barrier, len(peers))

    def tile_of(c):
        return pl.ds(pl.multiple_of(c * TILE, TILE), TILE)

    def send_p(i):
        return pltpu.make_async_remote_copy(
            src_ref=p_hbm, dst_ref=allp.at[pl.ds((i + 1) * rows, rows)],
            send_sem=p_send.at[i], recv_sem=p_recv.at[i], device_id=peers[i], device_id_type=MESH)

    def send_q(i, c):
        return pltpu.make_async_remote_copy(
            src_ref=q_hbm.at[tile_of(c)], dst_ref=qin.at[c, pl.ds(i * TILE, TILE)],
            send_sem=q_send.at[i, c], recv_sem=q_recv.at[i, c], device_id=peers[i], device_id_type=MESH)

    def send_lse(i):
        return pltpu.make_async_remote_copy(
            src_ref=lse_own, dst_ref=lse_in.at[i], send_sem=l_send.at[i], recv_sem=l_recv.at[i],
            device_id=peers[i], device_id_type=MESH)

    for i in (0, 1):
        send_p(i).start()
    for c in range(EARLY):
        for i in (0, 1):
            send_q(i, c).start()
    for load in loads:
        load.wait()

    def fold(tile, combine):
        return combine(tile.reshape(TILE // 8, 8, rows), axis=0)

    def scores(c, top):
        tile = nt(allp[tile_of(c)], q[...]) * scale
        s[tile_of(c)] = tile
        return jnp.maximum(top, fold(tile, jnp.max))

    def arrived_scores(c, top):
        for i in (0, 1):
            @pl.when(c == (i + 1) * n)
            def _():
                send_p(i).wait_recv()
        return scores(c, top)

    top = lax.fori_loop(0, 3 * n, arrived_scores, jnp.full((8, rows), -jnp.inf, jnp.float32))
    top = jnp.max(top, axis=0, keepdims=True)

    def add_up(c, total):
        return total + fold(jnp.exp(s[tile_of(c)] - top), jnp.sum)

    total = lax.fori_loop(0, 3 * n, add_up, jnp.zeros((8, rows), jnp.float32))
    lse = top + jnp.log(jnp.sum(total, axis=0, keepdims=True))
    lse_own[...] = jnp.broadcast_to(lse, lse_own.shape)
    for i in (0, 1):
        send_lse(i).start()
    for c in range(EARLY, n):
        for i in (0, 1):
            send_q(i, c).start()

    positive = pos[...]

    def weigh_own(c, picked):
        tile = s[tile_of(c)]
        hit = lax.broadcasted_iota(jnp.int32, tile.shape, 0) + c * TILE == positive
        w[tile_of(c)] = (jnp.exp(tile - lse) - hit.astype(jnp.float32)).astype(jnp.bfloat16)
        return picked + fold(jnp.where(hit, tile, 0.0), jnp.sum)

    def weigh(c, _):
        w[tile_of(c)] = jnp.exp(s[tile_of(c)] - lse).astype(jnp.bfloat16)
        return 0

    picked = lax.fori_loop(0, n, weigh_own, jnp.zeros((8, rows), jnp.float32))
    loss_ref[...] = lse - jnp.sum(picked, axis=0, keepdims=True)
    lax.fori_loop(n, 3 * n, weigh, 0)

    def local_grads(c, _):
        dq_ref[tile_of(c)] = tn(w[:, tile_of(c)], allp[...]).astype(jnp.bfloat16)
        own[tile_of(c)] = nn(w[tile_of(c)], q[...])
        return 0

    lax.fori_loop(0, n, local_grads, 0)
    for i in (0, 1):
        send_lse(i).wait_recv()

    def arrived(c, _):
        for i in (0, 1):
            send_q(i, c).wait_recv()
        lses = jnp.concatenate([lse_in[i, 0:1, tile_of(c)] for i in (0, 1)], axis=1)
        tile = nt(allp[0:rows], qin[c]) * scale
        w_in[...] = jnp.exp(tile - lses).astype(jnp.bfloat16)

        def add(j, _):
            span = pl.ds(pl.multiple_of(j * FIN, FIN), FIN)
            total = own[span] + nn(w_in[span], qin[c])
            own[span] = total
            dp_ref[span] = total.astype(jnp.bfloat16)
            return 0

        lax.fori_loop(0, rows // FIN, add, 0)
        return 0

    lax.fori_loop(0, n, arrived, 0)

    for i in (0, 1):
        send_p(i).wait_send()
        send_lse(i).wait_send()
        for c in range(n):
            send_q(i, c).wait_send()


def call_exchange(level, half, scale, queries, passages, positives):
    rows, width = queries.shape
    n = rows // TILE
    vmem, dma = pltpu.VMEM, pltpu.SemaphoreType.DMA
    f32, bf16 = jnp.float32, jnp.bfloat16
    outside = pl.BlockSpec(memory_space=pltpu.HBM)
    inside = pl.BlockSpec(memory_space=pltpu.VMEM)
    return pl.pallas_call(
        functools.partial(exchange, (half, 2**level), scale),
        out_shape=(vmem((1, rows), f32), vmem((rows, width), bf16), vmem((rows, width), bf16)),
        in_specs=[outside] * 3,
        out_specs=(inside,) * 3,
        scratch_shapes=[
            vmem((rows, width), bf16),
            vmem((1, rows), jnp.int32),
            vmem((3 * rows, width), bf16),
            vmem((n, 2 * TILE, width), bf16),
            vmem((3 * rows, rows), f32),
            vmem((3 * rows, rows), bf16),
            vmem((rows, 2 * TILE), bf16),
            vmem((rows, width), f32),
            vmem((8, rows), f32),
            vmem((2, 8, rows), f32),
            dma((3,)),
            dma((2,)),
            dma((2,)),
            dma((2, n)),
            dma((2, n)),
            dma((2,)),
            dma((2,)),
        ],
        name=f"exchange_{level}",
        cost_estimate=pl.CostEstimate(
            flops=22 * rows * rows * width, bytes_accessed=8 * rows * width, transcendentals=8 * rows * rows),
        compiler_params=pltpu.CompilerParams(
            collective_id=level, has_side_effects=True, vmem_limit_bytes=32 * 2**20),
    )(queries, passages, positives)


def write_out(loss, dq, dp, loss_hbm, dq_hbm, dp_hbm, sem):
    n = dq.shape[0] // TILE
    copies = [pltpu.make_async_copy(loss, loss_hbm, sem.at[2 * n])]
    for c in range(n):
        block = pl.ds(c * TILE, TILE)
        copies.append(pltpu.make_async_copy(dq.at[block], dq_hbm.at[block], sem.at[c]))
        copies.append(pltpu.make_async_copy(dp.at[block], dp_hbm.at[block], sem.at[n + c]))
    for copy in copies:
        copy.start()
    for copy in copies:
        copy.wait()


def call_write_out(*parts):
    outside = pl.BlockSpec(memory_space=pltpu.HBM)
    inside = pl.BlockSpec(memory_space=pltpu.VMEM)
    return pl.pallas_call(
        write_out,
        out_shape=tuple(jax.ShapeDtypeStruct(part.shape, part.dtype) for part in parts),
        in_specs=[inside] * 3,
        out_specs=(outside,) * 3,
        scratch_shapes=[pltpu.SemaphoreType.DMA((2 * (parts[1].shape[0] // TILE) + 1,))],
        name="write_out",
        compiler_params=pltpu.CompilerParams(vmem_limit_bytes=8 * 2**20),
    )(*parts)


def choose(half, levels, partners, index):
    other = partners[0, 0] ^ partners[1, 0] ^ half
    place = jnp.int32(0)
    for j in range(1, levels):
        place = place + (other >= 2**j).astype(jnp.int32)
    index[0] = place


def call_choose(half, levels, partners):
    return pl.pallas_call(
        functools.partial(choose, half, levels),
        out_shape=pltpu.SMEM((1,), jnp.int32),
        in_specs=[pl.BlockSpec(memory_space=pltpu.SMEM)],
        out_specs=pl.BlockSpec(memory_space=pltpu.SMEM),
        name="choose",
    )(partners)


def per_device(queries, passages, partners, positives):
    rows, width = queries.shape
    half = lax.axis_size("neg") // 2
    levels = half.bit_length() - 1
    index = call_choose(half, levels, partners)[0]
    branches = [functools.partial(call_exchange, level, half, width ** (-0.5)) for level in range(levels)]
    parts = lax.switch(index, branches, queries, passages, positives.reshape(1, rows))
    loss, grad_queries, grad_passages = call_write_out(*parts)
    return loss.reshape(rows), grad_queries, grad_passages


def solution(mesh):
    placed = (P(("dp", "neg"), None), P(("dp", "neg"), None), P(), P(("dp", "neg")))
    return jax.shard_map(
        per_device,
        mesh=mesh,
        in_specs=placed,
        out_specs=(P(("dp", "neg")), P(("dp", "neg"), None), P(("dp", "neg"), None)),
        check_vma=False,
    )
```

time: 198 us -> 204 us (1.030)
  the two profiles are of different devices: /device:TPU:24 before, /device:TPU:104 now
where the time goes in v3:
time: 204 us; the launch traced here: 203 us
  Pallas kernels  202 us (99%)
    pallas_call x1, Pallas kernels, call_exchange(): pl.pallas_call(functools.partial(exchange, (half, 2 ** level), scale), ou...  200 us

profile of v3, /device:TPU:104, one launch (start us, length us, event | category | flops | bytes accessed | tf_op | source)
XLA Modules:
  0.0 203.4 jit_solution(6923623267665245461)
XLA Ops:
  0.6 0.7 choose.1
  1.3 0.0 copy-start
  1.4 0.7 copy-done
  2.0 199.9 %conditional.1 = ((f32[1,512]{1,0:T(1,128)S(1)}, bf16[512,1024]{1,0:T(8,128)(2,1)S(1)}, bf16[512,1024]{1,0:T(8,128)(2,1)S(1)})) conditional(s32[]{:T(128)} %bitcast, (bf16[512,1024]{1,0:T(8,128)(2,1)}, bf16[512,1024]{1,0:T(8,128)(2,1)}, s32[1,512]{1,0:T(1,128)S(1)}) %tuple.40, (bf16[512,1024]{1,0:T(8,128)(2,1)}, ...), branch_computations={%region_0.0_spmd, %region_1.0_spmd, %region_2.0_spmd, %region_3.0_... | conditional | flops 5905580032 | bytes 4194312 | solution.py:245
  2.0 199.9 %exchange_3.1 = (f32[1,512]{1,0:T(1,128)S(1)}, bf16[512,1024]{1,0:T(8,128)(2,1)S(1)}, bf16[512,1024]{1,0:T(8,128)(2,1)S(1)}) custom-call(bf16[512,1024]{1,0:T(8,128)(2,1)} %get-tuple-element.45.q_hbm, bf16[512,1024]{1,0:T(8,128)(2,1)} %get-tuple-element.46.p_hbm, s32[1,512]{1,0:T(1,128)S(1)} %get-tuple-element.47.pos_hbm), custom_call_target="tpu_custom_call" | custom-call | flops 5905580032 | bytes 4194304 | tf_op jit(solution)/shard_map/cond/branch_3_fun/exchange_3/pallas_call | solution.py:162
  202.0 1.4 write_out.1
Async XLA Ops:
  1.3 0.7 copy-start

commit v4 on v3

--- a/solution.py
+++ b/solution.py
@@ -188,7 +188,7 @@
             flops=22 * rows * rows * width, bytes_accessed=8 * rows * width, transcendentals=8 * rows * rows),
         compiler_params=pltpu.CompilerParams(
             collective_id=level, has_side_effects=True, vmem_limit_bytes=32 * 2**20),
-    )(queries, passages, positives)
+    )(*[pltpu.with_memory_space_constraint(x, pltpu.HBM) for x in (queries, passages, positives)])
 
 
 def write_out(loss, dq, dp, loss_hbm, dq_hbm, dp_hbm, sem):

time: 204 us -> 55.6 us (0.27)
  the two profiles are of different devices: /device:TPU:104 before, /device:TPU:24 now
where the time goes in v4:
time: 55.6 us; the launch traced here: 54.6 us
  Pallas kernels  53.9 us (97%)
  between operations  0.65 us (1%)
    pallas_call x1, Pallas kernels, call_exchange(): pl.pallas_call(functools.partial(exchange, (half, 2 ** level), scale), ou...  51.8 us
    pallas_call x1, Pallas kernels, call_write_out(): pl.pallas_call(write_out, out_shape=tuple((jax.ShapeDtypeStruct(part.shap...  1.39 us

profile of v4, /device:TPU:24, one launch (start us, length us, event | category | flops | bytes accessed | tf_op | source)
XLA Modules:
  0.0 54.6 jit_solution(9017071718603561044)
XLA Ops:
  0.6 0.7 %choose.1 = s32[1]{0:T(128)S(4)} custom-call(s32[2,128]{1,0:T(2,128)} %partners.1), custom_call_target="tpu_custom_call" | custom-call | tf_op jit(solution)/shard_map/choose/pallas_call | solution.py:230
  1.3 51.8 %conditional.1 = ((f32[1,512]{1,0:T(1,128)S(1)}, bf16[512,1024]{1,0:T(8,128)(2,1)S(1)}, bf16[512,1024]{1,0:T(8,128)(2,1)S(1)})) conditional(s32[]{:T(128)} %bitcast, (bf16[512,1024]{1,0:T(8,128)(2,1)}, bf16[512,1024]{1,0:T(8,128)(2,1)}, s32[1,512]{1,0:T(1,128)}) %tuple.40, (bf16[512,1024]{1,0:T(8,128)(2,1)}, ...), branch_computations={%region_0.0_spmd, %region_1.0_spmd, %region_2.0_spmd, %region_3.0_... | conditional | flops 5905580032 | bytes 4194312 | solution.py:245
  1.4 51.8 %exchange_4.1 = (f32[1,512]{1,0:T(1,128)S(1)}, bf16[512,1024]{1,0:T(8,128)(2,1)S(1)}, bf16[512,1024]{1,0:T(8,128)(2,1)S(1)}) custom-call(bf16[512,1024]{1,0:T(8,128)(2,1)} %get-tuple-element.48.q_hbm, bf16[512,1024]{1,0:T(8,128)(2,1)} %get-tuple-element.49.p_hbm, s32[1,512]{1,0:T(1,128)} %get-tuple-element.50.pos_hbm), custom_call_target="tpu_custom_call" | custom-call | flops 5905580032 | bytes 4194304 | tf_op jit(solution)/shard_map/cond/branch_4_fun/exchange_4/pallas_call | solution.py:162
  53.2 1.4 %write_out.1 = (f32[1,512]{1,0:T(1,128)}, bf16[512,1024]{1,0:T(8,128)(2,1)}, bf16[512,1024]{1,0:T(8,128)(2,1)}) custom-call(f32[1,512]{1,0:T(1,128)S(1)} %get-tuple-element.63.loss, bf16[512,1024]{1,0:T(8,128)(2,1)S(1)} %get-tuple-element.64.dq, bf16[512,1024]{1,0:T(8,128)(2,1)S(1)} %get-tuple-element.65.dp), custom_call_target="tpu_custom_call" | custom-call | tf_op jit(solution)/shard_map/write_out/pallas_call | solution.py:210

commit v5 on v4

--- a/solution.py
+++ b/solution.py
@@ -10,7 +10,7 @@
 MESH = pl.DeviceIdType.MESH
 TILE = 128
 EARLY = 2
-FIN = 256
+HALF = 256
 
 
 def nt(left, right):
@@ -126,21 +126,19 @@
     for i in (0, 1):
         send_lse(i).wait_recv()
 
+    spans = [slice(j * HALF, (j + 1) * HALF) for j in range(rows // HALF)]
+
     def arrived(c, _):
         for i in (0, 1):
             send_q(i, c).wait_recv()
         lses = jnp.concatenate([lse_in[i, 0:1, tile_of(c)] for i in (0, 1)], axis=1)
-        tile = nt(allp[0:rows], qin[c]) * scale
-        w_in[...] = jnp.exp(tile - lses).astype(jnp.bfloat16)
-
-        def add(j, _):
-            span = pl.ds(pl.multiple_of(j * FIN, FIN), FIN)
+        for span in spans:
+            tile = nt(allp[span], qin[c]) * scale
+            w_in[span] = jnp.exp(tile - lses).astype(jnp.bfloat16)
+        for span in spans:
             total = own[span] + nn(w_in[span], qin[c])
             own[span] = total
             dp_ref[span] = total.astype(jnp.bfloat16)
-            return 0
-
-        lax.fori_loop(0, rows // FIN, add, 0)
         return 0
 
     lax.fori_loop(0, n, arrived, 0)

time: 55.6 us -> 197 us (3.54)
  Pallas kernels: 53.9 us -> 196 us
    pallas_call x1, Pallas kernels: 51.8 us -> 194 us  [call_exchange(): pl.pallas_call(functools.partial(exchange, (half, 2 ** level), scale), ou...]
where the time goes in v5:
time: 197 us
  Pallas kernels  196 us (99%)
    pallas_call x1, Pallas kernels, call_exchange(): pl.pallas_call(functools.partial(exchange, (half, 2 ** level), scale), ou...  194 us

profile of v5, /device:TPU:24, one launch (start us, length us, event | category | flops | bytes accessed | tf_op | source)
XLA Modules:
  0.0 196.6 jit_solution(8185114323797611674)
XLA Ops:
  0.6 0.7 choose.1
  1.3 193.9 %conditional.1 = ((f32[1,512]{1,0:T(1,128)S(1)}, bf16[512,1024]{1,0:T(8,128)(2,1)S(1)}, bf16[512,1024]{1,0:T(8,128)(2,1)S(1)})) conditional(s32[]{:T(128)} %bitcast, (bf16[512,1024]{1,0:T(8,128)(2,1)}, bf16[512,1024]{1,0:T(8,128)(2,1)}, s32[1,512]{1,0:T(1,128)}) %tuple.40, (bf16[512,1024]{1,0:T(8,128)(2,1)}, ...), branch_computations={%region_0.0_spmd, %region_1.0_spmd, %region_2.0_spmd, %region_3.0_... | conditional | flops 5905580032 | bytes 4194312 | solution.py:243
  1.4 193.8 %exchange_2.1 = (f32[1,512]{1,0:T(1,128)S(1)}, bf16[512,1024]{1,0:T(8,128)(2,1)S(1)}, bf16[512,1024]{1,0:T(8,128)(2,1)S(1)}) custom-call(bf16[512,1024]{1,0:T(8,128)(2,1)} %get-tuple-element.42.q_hbm, bf16[512,1024]{1,0:T(8,128)(2,1)} %get-tuple-element.43.p_hbm, s32[1,512]{1,0:T(1,128)} %get-tuple-element.44.pos_hbm), custom_call_target="tpu_custom_call" | custom-call | flops 5905580032 | bytes 4194304 | tf_op jit(solution)/shard_map/cond/branch_2_fun/exchange_2/pallas_call | solution.py:160
  195.2 1.4 write_out.1
